TPU v7x, 256 devices: a whole 4x4x8 slice. The times are simulated.
256 devices in a mesh: loop: 32 (over z, x_hi, core), bcast: 8 (over y, x_lo).
Axes of the slice: x: 4 (x_hi: 2, x_lo: 2; x = x_hi * 2 + x_lo), y: 4, z: 8, core: 2. Of those that a mesh axis runs over, the one named last changes fastest.
Arguments:
- s_blocks: float32 [32, 8, 1, 10, 256, 256], P('loop', 'bcast'), may hold values from -6 to 6
- s_list: int32 [32, 8, 1, 10, 2], P('loop', 'bcast'), may hold values from 0 to 3, as said below
- x_blocks: float32 [32, 8, 12, 256, 256], P('loop', 'bcast'), may hold values from -0.09375 to 0.09375
- x_list: int32 [32, 8, 12, 2], P('loop', 'bcast'), may hold values from 0 to 4, as said below
- c_list: int32 [32, 8, 10, 2], P('loop', 'bcast'), may hold values from 0 to 3, as said below
- owner: int32 [32, 4], P('loop'), may hold values from 0 to 7, as said below
Outputs:
- product: float32 [32, 8, 10, 256, 256], P('loop', 'bcast')
Inputs may be any that keep to these rules, and one draw needn't show every extreme that they name: `s_list`: positions within one list are distinct. `x_list`: positions within one list are distinct; entries with first value 4 are empty and stand after the occupied ones; some device's list has no empty entry. `c_list`: positions within one list are distinct. owner[l, s] = (s + q_l) mod 8 for a whole number q_l of each block-row group.
All inputs are finite; a program needn't handle non-finite values.
Results may differ from a plain program's by a relative error of at most 0.0003.
Values sent between devices are 32-bit elements; how exact they have to be, the bound alone decides.
A program may use at most 192 MiB of HBM per device.

v0:
```python
import jax
import jax.numpy as jnp
from jax import lax
from jax.sharding import PartitionSpec as P

RB = 3
KB = 4
CB = 4
STEPS = 4


HIGHEST = lax.Precision.HIGHEST


def shifted(shard, axis, by):
    length = lax.axis_size(axis)
    return lax.ppermute(shard, axis, [(i, (i + by) % length) for i in range(length)])


def spread(block, axis, owner):
    block = jnp.where(lax.axis_index(axis) == owner, block, jnp.zeros_like(block))
    return lax.psum(block, axis)


def densify(blocks, places, row_count, col_count):
    whole = places.astype(jnp.int32)
    chosen = (whole[:, 0][:, None, None] == jnp.arange(row_count)[None, :, None]) & (
        whole[:, 1][:, None, None] == jnp.arange(col_count)[None, None, :]
    )
    return jnp.einsum("irc,iab->rcab", chosen.astype(jnp.float32), blocks, precision=HIGHEST)


def block_terms(left, right, pairs):
    full_slab = jnp.einsum("rkab,kcbd->rcad", left, right, precision=HIGHEST)
    return full_slab[pairs[:, 0], pairs[:, 1]]


def per_device(s_blocks, s_list, x_blocks, x_list, c_list, owner):
    width = lax.axis_size("bcast")
    pairs = c_list[0, 0]
    resident = (x_blocks[0, 0], x_list[0, 0].astype(jnp.float32))
    current = resident
    total = jnp.zeros((pairs.shape[0], x_blocks.shape[3], x_blocks.shape[4]), jnp.float32)
    for step in range(STEPS):
        if step > 0:
            current = shifted((current[0], current[1]), "loop", -1)
        root = owner[0, step]
        slot = step // width
        left_blocks, left_places = (
            spread(s_blocks[0, 0, slot], "bcast", root),
            spread(s_list[0, 0, slot].astype(jnp.float32), "bcast", root),
        )
        left = densify(left_blocks, left_places, RB, KB)
        right = densify(current[0], current[1], KB, CB)
        total = total + block_terms(left, right, pairs)
    return total[None, None]


def solution(mesh):
    return jax.shard_map(
        per_device,
        mesh=mesh,
        in_specs=(
            P("loop", "bcast", None, None, None, None),
            P("loop", "bcast", None, None, None),
            P("loop", "bcast", None, None, None),
            P("loop", "bcast", None, None),
            P("loop", "bcast", None, None),
            P("loop", None),
        ),
        out_specs=P("loop", "bcast", None, None, None),
        check_vma=False,
    )
```

profile of v0, /device:TPU:1, one launch (start us, length us, event | category | flops | bytes accessed | tf_op | source)
XLA Modules:
  0.0 678.7 jit_solution(14331984064396226932)
XLA Ops:
  6.5 1.5 fusion.79
  10.5 6.0 select_bitcast_fusion.2
  16.5 1.9 copy-done.4
  18.4 3.2 collective-permute-start.1
  21.6 6.0 collective-permute-start
  27.7 42.8 %all-reduce = (f32[10,2]{0,1:T(2,128)S(1)}, f32[10,2]{0,1:T(2,128)S(1)}, f32[10,2]{0,1:T(2,128)S(1)}, f32[10,2]{0,1:T(2,128)S(1)}) all-reduce(f32[10,2]{0,1:T(2,128)S(1)} %get-tuple-element.37, f32[10,2]{0,1:T(2,128)S(1)} %get-tuple-element.36, f32[10,2]{0,1:T(2,128)S(1)} %get-tuple-element.38, ...), channel_id=1, replica_groups=mesh['loop'=32,'bcast'=8] {'bcast'}, use_global_device_ids=true, to_apply=%region_6.7 | all-reduce | flops 80 | bytes 640 | tf_op jit(solution)/shard_map/psum | solution.py:22
  70.5 33.0 %collective-permute-done.1 = f32[12,256,256]{2,1,0:T(8,128)} collective-permute-done((f32[12,256,256]{2,1,0:T(8,128)S(1)}, f32[12,256,256]{2,1,0:T(8,128)}, u32[]{:S(2)}, u32[]{:S(2)}) %collective-permute-start.1) | collective-permute-done | bytes 3145760 | tf_op jit(solution)/shard_map/ppermute | solution.py:17
  104.2 0.1 and_bitcast_fusion.4
  104.4 0.1 and_bitcast_fusion.3
  104.5 118.5 %collective-permute-done.3 = f32[12,256,256]{2,1,0:T(8,128)S(1)} collective-permute-done((f32[12,256,256]{2,1,0:T(8,128)}, f32[12,256,256]{2,1,0:T(8,128)S(1)}, u32[]{:S(2)}, u32[]{:S(2)}) %collective-permute-start.3) | collective-permute-done | bytes 3145760 | tf_op jit(solution)/shard_map/ppermute | solution.py:17
  223.1 6.2 fusion.32
  229.6 93.1 %collective-permute-done.2 = f32[12,2]{0,1:T(2,128)S(1)} collective-permute-done((f32[12,2]{0,1:T(2,128)S(1)}, f32[12,2]{0,1:T(2,128)S(1)}, u32[]{:S(2)}, u32[]{:S(2)}) %collective-permute-start.2) | collective-permute-done | bytes 128 | tf_op jit(solution)/shard_map/ppermute | solution.py:17
  322.7 0.4 collective-permute-start.4
  323.3 4.3 collective-permute-done.4
  327.8 8.3 %fusion.35 = f32[4,4,256,256,1]{3,1,2,0,4:T(4,128)} fusion(f32[12,256,256,1]{2,1,0,3:T(8,128)} %bitcast.23, pred[12,4,4,1]{2,1,0,3:T(4,128)(4,1)S(1)} %and_bitcast_fusion.2), kind=kOutput, calls=%fused_computation.42 | convolution fusion | flops 150994944 | bytes 7340224 | tf_op jit(solution)/shard_map/irc,iab->rcab/dot_general | solution.py:30
  336.1 6.2 fusion.38
  342.3 6.1 fusion.41
  348.5 200.5 %all-reduce.4.cloned.1.call-done = (f32[10,256,256]{2,1,0:T(8,128)}, f32[10,256,256]{2,1,0:T(8,128)}, f32[10,256,256]{2,1,0:T(8,128)}, f32[10,256,256]{2,1,0:T(8,128)}) async-done(((f32[10,256,256]{2,1,0:T(8,128)}, f32[10,256,256]{2,1,0:T(8,128)}, f32[10,256,256]{2,1,0:T(8,128)}, f32[10,256,256]{2,1,0:T(8,128)}), (f32[10,256,256]{2,1,0:T(8,128)}, f32[10,256,256]{2,1,0:T(8,128)}, f32[10,256,256]{2,1,0:T(8,128)}, ...) | async-done | bytes 10485776 | tf_op jit(solution)/shard_map/psum | solution.py:22
  548.9 6.2 fusion.8
  555.2 20.2 %fusion.59 = f32[3,4,256,256]{2,3,0,1:T(8,128)S(1)} fusion(f32[3,4,256,256]{3,1,2,0:T(4,128)S(1)} %fusion.8, f32[4,4,256,256,1]{3,1,2,0,4:T(4,128)S(1)} %copy-done.3), kind=kOutput, calls=%fused_computation.48 | convolution fusion | flops 9663676416 | bytes 10485760 | tf_op jit(solution)/shard_map/rkab,kcbd->rcad/dot_general | solution.py:34
  575.4 2.3 gather_fusion.3
  577.7 6.5 fusion.12
  584.2 20.2 %fusion.54 = f32[3,4,256,256]{2,3,0,1:T(8,128)S(1)} fusion(f32[3,4,256,256]{3,1,2,0:T(4,128)S(1)} %fusion.12, f32[4,4,256,256,1]{3,1,2,0,4:T(4,128)S(1)} %copy-done.2), kind=kOutput, calls=%fused_computation.47 | convolution fusion | flops 9663676416 | bytes 10485760 | tf_op jit(solution)/shard_map/rkab,kcbd->rcad/dot_general | solution.py:34
  604.4 2.4 gather_fusion.2
  606.8 6.3 fusion.16
  613.1 20.4 %fusion.49 = f32[3,4,256,256]{2,3,0,1:T(8,128)S(1)} fusion(f32[3,4,256,256]{3,1,2,0:T(4,128)S(1)} %fusion.16, f32[4,4,256,256,1]{3,1,2,0,4:T(4,128)S(1)} %copy-done.1), kind=kOutput, calls=%fused_computation.46 | convolution fusion | flops 9663676416 | bytes 10485760 | tf_op jit(solution)/shard_map/rkab,kcbd->rcad/dot_general | solution.py:34
  633.5 2.3 gather_fusion.1
  635.9 6.3 fusion.20
  642.1 20.2 %fusion.44 = f32[3,4,256,256]{2,3,0,1:T(8,128)S(1)} fusion(f32[3,4,256,256]{3,1,2,0:T(4,128)S(1)} %fusion.20, f32[4,4,256,256,1]{3,1,2,0,4:T(4,128)S(1)} %copy-done), kind=kOutput, calls=%fused_computation.45 | convolution fusion | flops 9663676416 | bytes 10485760 | tf_op jit(solution)/shard_map/rkab,kcbd->rcad/dot_general | solution.py:34
  662.4 2.3 gather_fusion
  664.7 4.9 add_bitcast_fusion
  669.6 2.1 copy.7
  (58 shorter events, 1.6 us)
Async XLA Ops:
  6.5 542.4 %all-reduce.4.cloned.1.call-start = ((), (), s32[]{:S(2)}) async-start(), calls=%async_computation | async-start | bytes 20971520 | tf_op jit(solution)/shard_map/psum | solution.py:22
  16.5 1.9 copy-start.4
  16.5 5.1 copy-start.5
  16.5 11.2 %copy-start.6 = (s32[1,1,1,10,2]{3,4,2,1,0:T(2,128)S(1)}, s32[1,1,1,10,2]{3,4,2,1,0:T(2,128)}, u32[]{:S(2)}) copy-start(s32[1,1,1,10,2]{3,4,2,1,0:T(2,128)} %param.7) | copy-start | bytes 244
  18.4 85.1 %collective-permute-start.1 = (f32[12,256,256]{2,1,0:T(8,128)S(1)}, f32[12,256,256]{2,1,0:T(8,128)}, u32[]{:S(2)}, u32[]{:S(2)}) collective-permute-start(f32[12,256,256]{2,1,0:T(8,128)S(1)} %bitcast.139), channel_id=1, source_target_pairs={{0,248},{8,0},{16,8},{24,16},{32,24},{40,32},{48,40},{56,48},{64,5... | collective-permute-start | bytes 9437192 | tf_op jit(solution)/shard_map/ppermute | solution.py:17
  21.6 207.7 %collective-permute-start = (f32[12,2]{0,1:T(2,128)S(1)}, f32[12,2]{0,1:T(2,128)S(1)}, u32[]{:S(2)}, u32[]{:S(2)}) collective-permute-start(f32[12,2]{0,1:T(2,128)S(1)} %get-tuple-element.24), channel_id=1, source_target_pairs={{0,248},{8,0},{16,8},{24,16},{32,24},{40,32},{48,40},{56,48},{64,5... | collective-permute-start | bytes 296 | tf_op jit(solution)/shard_map/ppermute | solution.py:17
  103.5 119.5 %collective-permute-start.3 = (f32[12,256,256]{2,1,0:T(8,128)}, f32[12,256,256]{2,1,0:T(8,128)S(1)}, u32[]{:S(2)}, u32[]{:S(2)}) collective-permute-start(f32[12,256,256]{2,1,0:T(8,128)} %collective-permute-done.1), channel_id=1, source_target_pairs={{0,248},{8,0},{16,8},{24,16},{32,24},{40,32},{48,40},{56,48},{64,5... | collective-permute-start | bytes 9437192 | tf_op jit(solution)/shard_map/ppermute | solution.py:17
  223.0 119.3 %collective-permute-start.5 = (f32[12,256,256]{2,1,0:T(8,128)S(1)}, f32[12,256,256]{2,1,0:T(8,128)S(1)}, u32[]{:S(2)}, u32[]{:S(2)}) collective-permute-start(f32[12,256,256]{2,1,0:T(8,128)S(1)} %collective-permute-done.3), channel_id=1, source_target_pairs={{0,248},{8,0},{16,8},{24,16},{32,24},{40,32},{48,40},{56,48},{64,5... | collective-permute-start | bytes 9437192 | tf_op jit(solution)/shard_map/ppermute | solution.py:17
  223.1 6.2 copy-start.7
  229.3 93.4 %collective-permute-start.2 = (f32[12,2]{0,1:T(2,128)S(1)}, f32[12,2]{0,1:T(2,128)S(1)}, u32[]{:S(2)}, u32[]{:S(2)}) collective-permute-start(f32[12,2]{0,1:T(2,128)S(1)} %collective-permute-done), channel_id=1, source_target_pairs={{0,248},{8,0},{16,8},{24,16},{32,24},{40,32},{48,40},{56,48},{64,5... | collective-permute-start | bytes 296 | tf_op jit(solution)/shard_map/ppermute | solution.py:17
  322.7 4.9 collective-permute-start.4
  548.9 6.3 copy-start.3
  577.7 6.5 copy-start.2
  606.8 6.3 copy-start.1
  635.9 6.3 copy-start
Sparse Core Ops, SparseCore 0:
  16.6 532.2 all-reduce.3
where the time goes:
time: 685 us; the launch traced here: 679 us
  waiting for transfers between devices  449 us (66%)
  matrix products  133 us (19%)
  blocking collectives  42.8 us (6%)
  between operations  16.4 us (2%)
  local copies, waits for them, and re-layouts  14.9 us (2%)
  other arithmetic  12.4 us (2%)
  starting transfers between devices  9.8 us (1%)
    ppermute x6, waiting for transfers between devices, shifted(): lax.ppermute(shard, axis, [(i, (i + by) % length) for i in range(length)])  249 us
    psum x1, waiting for transfers between devices, spread(): return lax.psum(block, axis)  200 us
    dot_general x4, matrix products, block_terms(): full_slab = jnp.einsum('rkab,kcbd->rcad', left, right, precision=HIGHEST)  81 us
    dot_general x8, matrix products, densify(): jnp.einsum('irc,iab->rcab', chosen.astype(jnp.float32), blocks, precision...  52.1 us
    psum x1, blocking collectives, spread(): return lax.psum(block, axis)  42.8 us
  transfers between devices with their start and end apart: 7, of which 5 were waited for; matrix products, arithmetic and copies ran while one was open for 4% of the time, Pallas kernels for 0%

commit v1 on v0

v1 whole, which is shorter than its diff:
```python
import jax
import jax.numpy as jnp
from jax import lax
from jax.experimental import pallas as pl
from jax.experimental.pallas import tpu as pltpu
from jax.sharding import PartitionSpec as P

RB = 3
KB = 4
CB = 4
STEPS = 4
NS = 10
NX = 12
NC = 10
NT = 4
NR = 2
HALF = NS // 2
MESH = pl.DeviceIdType.MESH
BF16 = jnp.bfloat16
F32 = jnp.float32


def kernel(meta_s, meta_v, s_hbm, x_hbm, o_hbm, *rest):
    lbufs = rest[:NT]
    (recv1, r_own, r_a, r_two, r_b, rd_hi, rd_lo, l_dense, acc, out_v, group_v, density_v,
     group_s, density_s, ss, rs, rss, rrs, ms, mr, own_sem, local_sem, out_sem) = rest[NT:]
    bs = s_hbm.shape[-1]
    tr = bs // NT
    n_loop, n_bcast = lax.axis_size("loop"), lax.axis_size("bcast")
    l, b = lax.axis_index("loop"), lax.axis_index("bcast")
    core = lax.rem(l, 2)
    hi_x = lax.rem(l // 2, 2)
    half = b // 4

    def loop_at(by):
        return (lax.rem(l + by + n_loop, n_loop), b)

    def bcast_at(by):
        return (l, lax.rem(b + by + n_bcast, n_bcast))

    def crossed(dev):
        return dev + 1 - 2 * lax.rem(dev, 2)

    def slot(dev):
        return 2 * lax.rem(dev, 4) + dev // 4

    across = (l, crossed(b))
    up, down = bcast_at(2), bcast_at(-2)
    sibling = (l + 1 - 2 * core, b)

    barrier = pltpu.get_barrier_semaphore()
    peers = [bcast_at(i) for i in range(1, 8)] + [loop_at(i) for i in (-3, -2, -1, 1, 2, 3)]
    for peer in peers:
        pl.semaphore_signal(barrier, inc=1, device_id=peer, device_id_type=MESH)
    pl.semaphore_wait(barrier, len(peers))

    def remote(src, dst, send_sem, recv_sem, dev):
        return pltpu.make_async_remote_copy(
            src_ref=src, dst_ref=dst, send_sem=send_sem, recv_sem=recv_sem, device_id=dev, device_id_type=MESH
        )

    def whole(t, dev):
        return lbufs[t].at[pl.ds(HALF * slot(dev), HALF)]

    def part(t, dev, j):
        return lbufs[t].at[pl.ds(HALF * slot(dev), HALF), pl.ds(j * (tr // 2), tr // 2)]

    left, right = down[1], up[1]

    def margin(t, kind):
        if kind == 0:
            src = s_hbm.at[pl.ds(HALF * (1 - half), HALF), pl.ds(t * tr, tr)]
            return remote(src, recv1.at[t], ss.at[t, 0], rs.at[t, 0], bcast_at(4))
        ref, dev = {
            1: (lambda: whole(t, b), across),
            2: (lambda: whole(t, b), up),
            3: (lambda: whole(t, b), down),
            4: (lambda: whole(t, across[1]), up),
            5: (lambda: whole(t, across[1]), down),
            6: (lambda: part(t, left, 0), up),
            7: (lambda: part(t, right, 1), down),
            8: (lambda: part(t, crossed(left), 0), up),
            9: (lambda: part(t, crossed(right), 1), down),
        }[kind]
        return remote(ref(), ref(), ss.at[t, kind], rs.at[t, kind], dev)

    xn = NX // NR

    def density(kind, j):
        at = pl.ds(j * xn, xn)
        dev, src, dst = {
            0: (loop_at(-2), x_hbm, r_two),
            1: ((lax.rem(l - 3 + 2 * core + n_loop, n_loop), b), x_hbm, r_a),
            2: (sibling, r_two, r_b),
        }[kind]
        return remote(src.at[at], dst.at[at], rss.at[kind, j], rrs.at[kind, j], dev)

    def relay(j):
        at = pl.ds(j * xn, xn)
        return remote(r_a.at[at], r_two.at[at], rss.at[3, j], rrs.at[0, j], loop_at(1))

    relays = jnp.logical_and(hi_x == 0, core == 1)
    direct = jnp.logical_not(jnp.logical_and(hi_x == 0, core == 0))

    def own_half(t):
        src = s_hbm.at[pl.ds(HALF * half, HALF), pl.ds(t * tr, tr)]
        return pltpu.make_async_copy(src, whole(t, b), own_sem.at[t])

    for j in range(NR):
        density(1, j).start()
    margin(0, 0).start()
    own_half(0).start()

    @pl.when(direct)
    def _():
        for j in range(NR):
            density(0, j).start()

    own_density = pltpu.make_async_copy(x_hbm, r_own, local_sem.at[0])
    own_density.start()
    for t in range(1, NT):
        margin(t, 0).start()
        own_half(t).start()

    def table(i):
        if i < 7:
            return remote(meta_v, group_v.at[b], ms.at[i], mr.at[i], bcast_at(i + 1))
        by = i - 6
        return remote(meta_v, density_v.at[by], ms.at[i], mr.at[i], loop_at(-by))

    for i in range(10):
        table(i).start()
    mine_g = pltpu.make_async_copy(meta_v, group_v.at[b], local_sem.at[1])
    mine_d = pltpu.make_async_copy(meta_v, density_v.at[0], local_sem.at[2])
    mine_g.start()
    mine_d.start()

    def split(block):
        high = block.astype(BF16)
        return high, (block - high.astype(F32)).astype(BF16)

    def spread_density(ref, j, step):
        def body(i, carry):
            k, c = i // CB, lax.rem(i, CB)
            at = density_s[step, 0, 16 + i]
            block = jnp.where(at < NX, ref[jnp.minimum(at, NX - 1)], 0.0)
            rows = pl.ds(pl.multiple_of(k * bs, bs), bs)
            high, low = split(block)
            rd_hi[j, c, rows, :] = high
            rd_lo[j, c, rows, :] = low
            return carry

        lax.fori_loop(0, KB * CB, body, 0)

    wanted = (meta_s[0, 48] == b) | (meta_s[0, 49] == b) | (meta_s[0, 50] == b) | (meta_s[0, 51] == b)

    def choose(t):
        margin(t, 0).wait_recv()
        own_half(t).wait()

        def body(i, carry):
            at = HALF * slot(b) + i
            lbufs[t][at] = jnp.where(wanted, lbufs[t][at], recv1[t, i])
            return carry

        lax.fori_loop(0, HALF, body, 0)
        for kind in (1, 2, 3):
            margin(t, kind).start()

    def cross(t):
        margin(t, 1).wait_recv()
        for kind in (4, 5):
            margin(t, kind).start()

    def forward(t):
        for kind in (2, 3, 4, 5):
            margin(t, kind).wait_recv()
            margin(t, kind + 4).start()

    def finish(t):
        for kind in (6, 7, 8, 9):
            margin(t, kind).wait_recv()

    step_of = (0, 1 + 2 * core, 2, 3 - 2 * core)

    def spread_margin(t):
        for j in range(STEPS):
            root = meta_s[0, 48 + step_of[j]]

            def body(i, carry):
                r, k = i // KB, lax.rem(i, KB)
                at = group_s[root, 0, i]
                block = lbufs[t][NS * lax.rem(root, 4) + jnp.minimum(at, NS - 1)]
                high, low = split(jnp.where(at < NS, block, 0.0))
                cols = pl.ds(pl.multiple_of(k * bs, bs), bs)
                l_dense[j, pl.ds(pl.multiple_of(r * tr, tr), tr), cols] = high
                l_dense[j, pl.ds(pl.multiple_of((RB + r) * tr, tr), tr), cols] = low
                return carry

            lax.fori_loop(0, RB * KB, body, 0)

    def multiply(t):
        def column(c, carry):
            total = jnp.zeros((RB * tr, bs), F32)
            for j in range(STEPS):
                first = jnp.dot(l_dense[j], rd_hi[j, c], preferred_element_type=F32)
                second = jnp.dot(l_dense[j, : RB * tr, :], rd_lo[j, c], preferred_element_type=F32)
                total = total + (first[: RB * tr] + (first[RB * tr :] + second))
            for r in range(RB):
                acc[r * CB + c] = total[r * tr : (r + 1) * tr]
            return carry

        lax.fori_loop(0, CB, column, 0)

        def keep(m, carry):
            out_v[m, t * tr : (t + 1) * tr, :] = acc[meta_s[0, 64 + m]]
            return carry

        lax.fori_loop(0, NC, keep, 0)
        out(t).start()

    def out(t):
        at = pl.ds(t * tr, tr)
        return pltpu.make_async_copy(out_v.at[:, at], o_hbm.at[:, at], out_sem.at[t])

    choose(0)
    for i in range(10):
        table(i).wait_recv()
    mine_g.wait()
    mine_d.wait()
    to_s = [
        pltpu.make_async_copy(group_v, group_s, local_sem.at[3]),
        pltpu.make_async_copy(density_v, density_s, local_sem.at[4]),
    ]
    for copy in to_s:
        copy.start()
    choose(1)
    cross(0)
    for copy in to_s:
        copy.wait()
    own_density.wait()
    spread_density(r_own, 0, 0)
    choose(2)
    cross(1)
    forward(0)

    for j in range(NR):
        density(1, j).wait_recv()

        @pl.when(relays)
        def _():
            relay(j).start()

    spread_density(r_a, 1, step_of[1])
    choose(3)
    cross(2)
    forward(1)
    cross(3)
    finish(0)
    for j in range(NR):
        density(0, j).wait_recv()
        density(2, j).start()
    spread_density(r_two, 2, 2)
    forward(2)
    spread_margin(0)
    for j in range(NR):
        density(2, j).wait_recv()
    spread_density(r_b, 3, step_of[3])
    forward(3)
    multiply(0)
    for t in range(1, NT):
        finish(t)
        spread_margin(t)
        multiply(t)

    for t in range(NT):
        out(t).wait()
        for kind in range(10):
            margin(t, kind).wait_send()
    for j in range(NR):
        density(1, j).wait_send()
        density(2, j).wait_send()

    @pl.when(direct)
    def _():
        for j in range(NR):
            density(0, j).wait_send()

    @pl.when(relays)
    def _():
        for j in range(NR):
            relay(j).wait_send()

    for i in range(10):
        table(i).wait_send()


def tables(s_list, x_list, c_list, owner):
    def inverse(places, columns, cells, empty):
        cell = places[:, 0] * columns + places[:, 1]
        match = cell[:, None] == jnp.arange(cells)[None, :]
        return jnp.min(jnp.where(match, jnp.arange(places.shape[0])[:, None], empty), axis=0)

    def padded(row, size):
        return jnp.pad(row, (0, size - row.shape[0]))

    row = jnp.concatenate([
        padded(inverse(s_list, KB, RB * KB, NS), 16),
        padded(inverse(x_list, CB, KB * CB, NX), 32),
        padded(owner, 16),
        padded(c_list[:, 0] * CB + c_list[:, 1], 64),
    ])
    return jnp.broadcast_to(row.astype(jnp.int32)[None], (8, 128))


def per_device(s_blocks, s_list, x_blocks, x_list, c_list, owner):
    bs = s_blocks.shape[-1]
    tr = bs // NT
    meta = tables(s_list[0, 0, 0], x_list[0, 0], c_list[0, 0], owner[0])
    any_spec = pl.BlockSpec(memory_space=pl.ANY)
    hbm = pl.BlockSpec(memory_space=pltpu.HBM)
    product = pl.pallas_call(
        kernel,
        out_shape=jax.ShapeDtypeStruct((NC, bs, bs), F32),
        in_specs=[pl.BlockSpec(memory_space=pltpu.SMEM), pl.BlockSpec(memory_space=pltpu.VMEM), hbm, hbm],
        out_specs=hbm,
        scratch_shapes=[pltpu.VMEM((4 * NS, tr, bs), F32)] * NT + [
            pltpu.VMEM((NT, HALF, tr, bs), F32),
            pltpu.VMEM((NX, bs, bs), F32),
            pltpu.VMEM((NX, bs, bs), F32),
            pltpu.VMEM((NX, bs, bs), F32),
            pltpu.VMEM((NX, bs, bs), F32),
            pltpu.VMEM((STEPS, CB, KB * bs, bs), BF16),
            pltpu.VMEM((STEPS, CB, KB * bs, bs), BF16),
            pltpu.VMEM((STEPS, 2 * RB * tr, KB * bs), BF16),
            pltpu.VMEM((RB * CB, tr, bs), F32),
            pltpu.VMEM((NC, bs, bs), F32),
            pltpu.VMEM((8, 8, 128), jnp.int32),
            pltpu.VMEM((4, 8, 128), jnp.int32),
            pltpu.SMEM((8, 8, 128), jnp.int32),
            pltpu.SMEM((4, 8, 128), jnp.int32),
            pltpu.SemaphoreType.DMA((NT, 10)),
            pltpu.SemaphoreType.DMA((NT, 10)),
            pltpu.SemaphoreType.DMA((4, NR)),
            pltpu.SemaphoreType.DMA((3, NR)),
            pltpu.SemaphoreType.DMA((10,)),
            pltpu.SemaphoreType.DMA((10,)),
            pltpu.SemaphoreType.DMA((NT,)),
            pltpu.SemaphoreType.DMA((5,)),
            pltpu.SemaphoreType.DMA((NT,)),
        ],
        compiler_params=pltpu.CompilerParams(
            collective_id=0, has_side_effects=True, vmem_limit_bytes=60 * 1024 * 1024
        ),
        cost_estimate=pl.CostEstimate(flops=20 * 10**9, bytes_accessed=10**7, transcendentals=0),
    )(meta, meta, s_blocks[0, 0, 0], x_blocks[0, 0])
    return product[None, None]


def solution(mesh):
    return jax.shard_map(
        per_device,
        mesh=mesh,
        in_specs=(
            P("loop", "bcast", None, None, None, None),
            P("loop", "bcast", None, None, None),
            P("loop", "bcast", None, None, None),
            P("loop", "bcast", None, None),
            P("loop", "bcast", None, None),
            P("loop", None),
        ),
        out_specs=P("loop", "bcast", None, None, None),
        check_vma=False,
    )
```

time: 685 us -> 184 us (0.27)
  waiting for transfers between devices: 449 us -> 0 us
  Pallas kernels: 0 us -> 176 us
  matrix products: 133 us -> 0 us
  blocking collectives: 42.8 us -> 0 us
  between operations: 16.4 us -> 0.01 us
  local copies, waits for them, and re-layouts: 14.9 us -> 4.02 us
  starting transfers between devices: 9.8 us -> 0 us
  other arithmetic: 12.4 us -> 3.18 us
    ppermute x6 -> x0, waiting for transfers between devices: 249 us -> none  [shifted(): lax.ppermute(shard, axis, [(i, (i + by) % length) for i in range(length)])]
    psum x1 -> x0, waiting for transfers between devices: 200 us -> none  [spread(): return lax.psum(block, axis)]
    pallas_call x0 -> x1, Pallas kernels: none -> 176 us  [per_device(): pl.pallas_call(kernel, out_shape=jax.ShapeDtypeStruct((NC, bs, bs), F32),...]
    dot_general x12 -> x0, matrix products: 133 us -> none  [the longest x4 81 us: block_terms(): full_slab = jnp.einsum('rkab,kcbd->rcad', left, right, precision=HIGHEST)]
    psum x1 -> x0, blocking collectives: 42.8 us -> none  [spread(): return lax.psum(block, axis)]
    ppermute x6 -> x0, starting transfers between devices: 9.8 us -> none  [shifted(): lax.ppermute(shard, axis, [(i, (i + by) % length) for i in range(length)])]
    gather x4 -> x0, local copies, waits for them, and re-layouts: 9.38 us -> none  [block_terms(): return full_slab[pairs[:, 0], pairs[:, 1]]]
  transfers between devices with their start and end apart: 7 -> 0, of which waited for: 5 -> 0; matrix products, arithmetic and copies ran while one was open for 4% -> 0% of each run, Pallas kernels for 0% -> 0%
where the time goes in v1:
time: 184 us
  Pallas kernels  176 us (96%)
  local copies, waits for them, and re-layouts  4.02 us (2%)
  other arithmetic  3.18 us (2%)
    pallas_call x1, Pallas kernels, per_device(): pl.pallas_call(kernel, out_shape=jax.ShapeDtypeStruct((NC, bs, bs), F32),...  176 us

profile of v1, /device:TPU:1, one launch (start us, length us, event | category | flops | bytes accessed | tf_op | source)
XLA Modules:
  0.0 183.5 jit_solution(8042480462954936555)
XLA Ops:
  0.0 0.8 add_bitcast_fusion.2
  0.8 0.1 select_reduce_fusion.1
  0.8 0.8 add_bitcast_fusion.1
  1.6 0.1 select_reduce_fusion
  1.7 0.8 add_bitcast_fusion
  2.5 0.7 pad_add_fusion
  3.2 0.6 broadcast_in_dim.43.meta_s.meta_v
  3.8 176.3 %shard_map.64 = f32[10,256,256]{2,1,0:T(8,128)} custom-call(s32[8,128]{1,0:T(8,128)} %broadcast_in_dim.43.meta_s.meta_v, s32[8,128]{1,0:T(8,128)} %broadcast_in_dim.43.meta_s.meta_v, f32[10,256,256]{2,1,0:T(8,128)} %bitcast.16, f32[12,256,256]{2,1,0:T(8,128)} %bitcast.15), custom_call_target="tpu_custom_call" | custom-call | flops 20000000000 | bytes 10000000 | tf_op jit(solution)/shard_map/pallas_call | solution.py:322
  180.1 3.4 %copy.8 = f32[1,1,10,256,256]{4,3,2,1,0:T(8,128)} copy(f32[1,1,10,256,256]{4,3,2,1,0:T(8,128)} %bitcast.13) | data formatting | bytes 5242880

commit v2 on v1

v2 whole, which is shorter than its diff:
```python
import jax
import jax.numpy as jnp
from jax import lax
from jax.experimental import pallas as pl
from jax.experimental.pallas import tpu as pltpu
from jax.sharding import PartitionSpec as P

RB = 3
KB = 4
CB = 4
STEPS = 4
NS = 10
NX = 12
NC = 10
NT = 4
ND = 6
NR = 3
HALF = NS // 2
MESH = pl.DeviceIdType.MESH
BF16 = jnp.bfloat16
F32 = jnp.float32


def kernel(c_s, owner_s, s_places, x_places, s_hbm, x_hbm, o_hbm, *rest):
    lbufs = rest[:NT]
    (recv1, r_own, r_a, r_two, r_b, rd_hi, rd_lo, l_dense, acc, out_v, meta_v, group_v, density_v,
     group_s, density_s, ss, rs, rss, rrs, dss, drs, pss, prs, ms, mr, own_sem, local_sem, out_sem) = rest[NT:]
    bs = s_hbm.shape[-1]
    tr = bs // NT
    n_loop, n_bcast = lax.axis_size("loop"), lax.axis_size("bcast")
    l, b = lax.axis_index("loop"), lax.axis_index("bcast")
    core = lax.rem(l, 2)
    hi_x = lax.rem(l // 2, 2)
    half = b // 4

    def loop_at(by):
        return (lax.rem(l + by + n_loop, n_loop), b)

    def bcast_at(by):
        return (l, lax.rem(b + by + n_bcast, n_bcast))

    def crossed(dev):
        return dev + 1 - 2 * lax.rem(dev, 2)

    def slot(dev):
        return 2 * lax.rem(dev, 4) + dev // 4

    across = (l, crossed(b))
    up, down = bcast_at(2), bcast_at(-2)
    sibling = (l + 1 - 2 * core, b)

    def stands(places, columns, count):
        cell = places[0:1, :] * columns + places[1:2, :]
        position = lax.broadcasted_iota(jnp.int32, (KB * CB, count), 0)
        entry = lax.broadcasted_iota(jnp.int32, (KB * CB, count), 1)
        return jnp.min(jnp.where(cell == position, entry, count), axis=1, keepdims=True)

    lane = lax.broadcasted_iota(jnp.int32, (KB * CB, 128), 1)
    meta_v[...] = jnp.where(lane == 0, stands(s_places, KB, NS), stands(x_places, CB, NX))

    barrier = pltpu.get_barrier_semaphore()
    peers = [bcast_at(i) for i in range(1, 8)] + [loop_at(i) for i in (-3, -2, -1, 1, 2, 3)]
    for peer in peers:
        pl.semaphore_signal(barrier, inc=1, device_id=peer, device_id_type=MESH)
    pl.semaphore_wait(barrier, len(peers))

    def remote(src, dst, send_sem, recv_sem, dev):
        return pltpu.make_async_remote_copy(
            src_ref=src, dst_ref=dst, send_sem=send_sem, recv_sem=recv_sem, device_id=dev, device_id_type=MESH
        )

    def whole(t, dev):
        return lbufs[t].at[pl.ds(HALF * slot(dev), HALF)]

    def part(t, dev, j):
        return lbufs[t].at[pl.ds(HALF * slot(dev), HALF), pl.ds(j * (tr // 2), tr // 2)]

    left, right = down[1], up[1]

    def margin(t, kind):
        if kind == 0:
            src = s_hbm.at[pl.ds(HALF * (1 - half), HALF), pl.ds(t * tr, tr)]
            return remote(src, recv1.at[t], ss.at[t, 0], rs.at[t, 0], bcast_at(4))
        ref, dev = {
            1: (lambda: whole(t, b), across),
            2: (lambda: whole(t, b), up),
            3: (lambda: whole(t, b), down),
            4: (lambda: whole(t, across[1]), up),
            5: (lambda: whole(t, across[1]), down),
            6: (lambda: part(t, left, 0), up),
            7: (lambda: part(t, right, 1), down),
            8: (lambda: part(t, crossed(left), 0), up),
            9: (lambda: part(t, crossed(right), 1), down),
        }[kind]
        return remote(ref(), ref(), ss.at[t, kind], rs.at[t, kind], dev)

    xn = NX // NR

    lower = (lax.rem(l - 3 + 2 * core + n_loop, n_loop), b)

    def density(kind):
        dev, src, dst = {
            1: (lower, x_hbm, r_a),
            2: (sibling, r_two, r_b),
        }[kind]
        return remote(src, dst, rss.at[kind], rrs.at[kind], dev)

    def direct(k):
        at = pl.ds(k * (NX // ND), NX // ND)
        return remote(x_hbm.at[at], r_two.at[at], dss.at[k], drs.at[k], loop_at(-2))

    def relayed(j):
        at = pl.ds(j * xn, xn)
        return remote(x_hbm.at[at], r_a.at[at], pss.at[0, j], prs.at[0, j], lower)

    def relay(j):
        at = pl.ds(j * xn, xn)
        return remote(r_a.at[at], r_two.at[at], pss.at[1, j], prs.at[1, j], loop_at(1))

    gives = jnp.logical_and(hi_x == 0, core == 0)
    relays = jnp.logical_and(hi_x == 0, core == 1)
    takes = jnp.logical_and(hi_x == 1, core == 0)

    def either(flag, then, otherwise):
        pl.when(flag)(then)
        pl.when(jnp.logical_not(flag))(otherwise)

    def own_half(t):
        src = s_hbm.at[pl.ds(HALF * half, HALF), pl.ds(t * tr, tr)]
        return pltpu.make_async_copy(src, whole(t, b), own_sem.at[t])

    def begin(t):
        margin(t, 0).start()
        own_half(t).start()

    def table(i):
        if i < 7:
            return remote(meta_v, group_v.at[b], ms.at[i], mr.at[i], bcast_at(i + 1))
        by = i - 6
        return remote(meta_v, density_v.at[by], ms.at[i], mr.at[i], loop_at(-by))

    for i in range(10):
        table(i).start()
    mine_g = pltpu.make_async_copy(meta_v, group_v.at[b], local_sem.at[1])
    mine_d = pltpu.make_async_copy(meta_v, density_v.at[0], local_sem.at[2])
    mine_g.start()
    mine_d.start()

    begin(0)
    either(gives, lambda: relayed(0).start(), lambda: density(1).start())

    @pl.when(jnp.logical_not(gives))
    def _():
        direct(0).start()
        direct(1).start()

    begin(1)
    own_density = pltpu.make_async_copy(x_hbm, r_own, local_sem.at[0])
    own_density.start()

    def split(block):
        high = block.astype(BF16)
        return high, (block - high.astype(F32)).astype(BF16)

    def spread_density(ref, j, step):
        def body(i, carry):
            k, c = i // CB, lax.rem(i, CB)
            at = density_s[step, i, 1]
            block = jnp.where(at < NX, ref[jnp.minimum(at, NX - 1)], 0.0)
            rows = pl.ds(pl.multiple_of(k * bs, bs), bs)
            high, low = split(block)
            rd_hi[j, c, rows, :] = high
            rd_lo[j, c, rows, :] = low
            return carry

        lax.fori_loop(0, KB * CB, body, 0)

    wanted = (owner_s[0, 0] == b) | (owner_s[0, 1] == b) | (owner_s[0, 2] == b) | (owner_s[0, 3] == b)

    def choose(t):
        margin(t, 0).wait_recv()
        own_half(t).wait()

        def body(i, carry):
            at = HALF * slot(b) + i
            lbufs[t][at] = jnp.where(wanted, lbufs[t][at], recv1[t, i])
            return carry

        lax.fori_loop(0, HALF, body, 0)
        for kind in (1, 2, 3):
            margin(t, kind).start()

    def cross(t):
        margin(t, 1).wait_recv()
        for kind in (4, 5):
            margin(t, kind).start()

    def forward_own(t):
        for kind in (2, 3):
            margin(t, kind).wait_recv()
            margin(t, kind + 4).start()

    def forward_crossed(t):
        for kind in (4, 5):
            margin(t, kind).wait_recv()
            margin(t, kind + 4).start()

    def finish(t):
        for kind in (6, 7, 8, 9):
            margin(t, kind).wait_recv()

    def advance(k):
        @pl.when(jnp.logical_not(gives))
        def _():
            direct(k).wait_send()
            direct(k + 2).start()

    def density_turn(j):
        if j + 1 < NR:

            @pl.when(gives)
            def _():
                relayed(j).wait_send()
                relayed(j + 1).start()

        @pl.when(relays)
        def _():
            relayed(j).wait_recv()
            relay(j).start()

    step_of = (0, 1 + 2 * core, 2, 3 - 2 * core)

    def spread_margin(t):
        for j in range(STEPS):
            root = owner_s[0, step_of[j]]

            def body(i, carry):
                r, k = i // KB, lax.rem(i, KB)
                at = group_s[root, i, 0]
                block = lbufs[t][NS * lax.rem(root, 4) + jnp.minimum(at, NS - 1)]
                high, low = split(jnp.where(at < NS, block, 0.0))
                cols = pl.ds(pl.multiple_of(k * bs, bs), bs)
                l_dense[t % 2, j, pl.ds(pl.multiple_of(r * tr, tr), tr), cols] = high
                l_dense[t % 2, j, pl.ds(pl.multiple_of((RB + r) * tr, tr), tr), cols] = low
                return carry

            lax.fori_loop(0, RB * KB, body, 0)

    def multiply(t, terms):
        def column(c, carry):
            total = jnp.zeros((RB * tr, bs), F32)
            for j in terms:
                first = jnp.dot(l_dense[t % 2, j], rd_hi[j, c], preferred_element_type=F32)
                second = jnp.dot(l_dense[t % 2, j, : RB * tr, :], rd_lo[j, c], preferred_element_type=F32)
                total = total + (first[: RB * tr] + (first[RB * tr :] + second))
            for r in range(RB):
                piece = total[r * tr : (r + 1) * tr]
                acc[t, r * CB + c] = piece if terms[0] == 0 else acc[t, r * CB + c] + piece
            return carry

        lax.fori_loop(0, CB, column, 0)

    def keep(t):
        def body(m, carry):
            out_v[m, t * tr : (t + 1) * tr, :] = acc[t, c_s[0, m] * CB + c_s[1, m]]
            return carry

        lax.fori_loop(0, NC, body, 0)
        out(t).start()

    def out(t):
        at = pl.ds(t * tr, tr)
        return pltpu.make_async_copy(out_v.at[:, at], o_hbm.at[:, at], out_sem.at[t])

    for i in range(10):
        table(i).wait_recv()
    mine_g.wait()
    mine_d.wait()
    to_s = [
        pltpu.make_async_copy(group_v, group_s, local_sem.at[3]),
        pltpu.make_async_copy(density_v, density_s, local_sem.at[4]),
    ]
    for copy in to_s:
        copy.start()
    choose(0)
    begin(2)
    advance(0)
    choose(1)
    begin(3)
    for copy in to_s:
        copy.wait()
    cross(0)
    density_turn(0)
    advance(1)
    forward_own(0)
    choose(2)
    cross(1)
    own_density.wait()
    spread_density(r_own, 0, 0)
    advance(2)
    forward_crossed(0)
    density_turn(1)
    forward_own(1)
    choose(3)
    cross(2)
    advance(3)
    forward_crossed(1)
    density_turn(2)
    forward_own(2)
    finish(0)
    cross(3)
    pl.when(jnp.logical_not(relays))(lambda: density(1).wait_recv())
    spread_density(r_a, 1, step_of[1])
    forward_crossed(2)
    forward_own(3)
    spread_margin(0)
    multiply(0, (0, 1))
    finish(1)
    forward_crossed(3)
    spread_margin(1)
    multiply(1, (0, 1))

    def parts_in():
        for j in range(NR):
            relay(j).wait_recv()

    def direct_in():
        for k in range(ND):
            direct(k).wait_recv()

    either(takes, parts_in, direct_in)
    density(2).start()
    spread_density(r_two, 2, 2)
    density(2).wait_recv()
    spread_density(r_b, 3, step_of[3])
    multiply(0, (2, 3))
    keep(0)
    multiply(1, (2, 3))
    keep(1)
    for t in range(2, NT):
        finish(t)
        spread_margin(t)
        multiply(t, (0, 1, 2, 3))
        keep(t)

    for t in range(NT):
        out(t).wait()
        for kind in range(10):
            margin(t, kind).wait_send()
    density(2).wait_send()

    def sent():
        density(1).wait_send()
        for k in range(ND - 2, ND):
            direct(k).wait_send()

    either(gives, lambda: relayed(NR - 1).wait_send(), sent)

    @pl.when(relays)
    def _():
        for j in range(NR):
            relay(j).wait_send()

    for i in range(10):
        table(i).wait_send()


def per_device(s_blocks, s_list, x_blocks, x_list, c_list, owner):
    bs = s_blocks.shape[-1]
    tr = bs // NT
    smem = pl.BlockSpec(memory_space=pltpu.SMEM)
    vmem = pl.BlockSpec(memory_space=pltpu.VMEM)
    hbm = pl.BlockSpec(memory_space=pltpu.HBM)
    product = pl.pallas_call(
        kernel,
        out_shape=jax.ShapeDtypeStruct((NC, bs, bs), F32),
        in_specs=[smem, smem, vmem, vmem, hbm, hbm],
        out_specs=hbm,
        scratch_shapes=[pltpu.VMEM((4 * NS, tr, bs), F32)] * NT + [
            pltpu.VMEM((NT, HALF, tr, bs), F32),
            pltpu.VMEM((NX, bs, bs), F32),
            pltpu.VMEM((NX, bs, bs), F32),
            pltpu.VMEM((NX, bs, bs), F32),
            pltpu.VMEM((NX, bs, bs), F32),
            pltpu.VMEM((STEPS, CB, KB * bs, bs), BF16),
            pltpu.VMEM((STEPS, CB, KB * bs, bs), BF16),
            pltpu.VMEM((2, STEPS, 2 * RB * tr, KB * bs), BF16),
            pltpu.VMEM((NT, RB * CB, tr, bs), F32),
            pltpu.VMEM((NC, bs, bs), F32),
            pltpu.VMEM((KB * CB, 128), jnp.int32),
            pltpu.VMEM((8, KB * CB, 128), jnp.int32),
            pltpu.VMEM((4, KB * CB, 128), jnp.int32),
            pltpu.SMEM((8, KB * CB, 128), jnp.int32),
            pltpu.SMEM((4, KB * CB, 128), jnp.int32),
            pltpu.SemaphoreType.DMA((NT, 10)),
            pltpu.SemaphoreType.DMA((NT, 10)),
            pltpu.SemaphoreType.DMA((3,)),
            pltpu.SemaphoreType.DMA((3,)),
            pltpu.SemaphoreType.DMA((ND,)),
            pltpu.SemaphoreType.DMA((ND,)),
            pltpu.SemaphoreType.DMA((2, NR)),
            pltpu.SemaphoreType.DMA((2, NR)),
            pltpu.SemaphoreType.DMA((10,)),
            pltpu.SemaphoreType.DMA((10,)),
            pltpu.SemaphoreType.DMA((NT,)),
            pltpu.SemaphoreType.DMA((5,)),
            pltpu.SemaphoreType.DMA((NT,)),
        ],
        compiler_params=pltpu.CompilerParams(
            collective_id=0, has_side_effects=True, vmem_limit_bytes=60 * 1024 * 1024
        ),
        cost_estimate=pl.CostEstimate(flops=20 * 10**9, bytes_accessed=10**7, transcendentals=0),
    )(c_list[0, 0].T, owner, s_list[0, 0, 0].T, x_list[0, 0].T, s_blocks[0, 0, 0], x_blocks[0, 0])
    return product[None, None]


def solution(mesh):
    return jax.shard_map(
        per_device,
        mesh=mesh,
        in_specs=(
            P("loop", "bcast", None, None, None, None),
            P("loop", "bcast", None, None, None),
            P("loop", "bcast", None, None, None),
            P("loop", "bcast", None, None),
            P("loop", "bcast", None, None),
            P("loop", None),
        ),
        out_specs=P("loop", "bcast", None, None, None),
        check_vma=False,
    )
```

time: 184 us -> 154 us (0.84)
  Pallas kernels: 176 us -> 150 us
  other arithmetic: 3.18 us -> 0 us
    pallas_call x1, Pallas kernels: 176 us -> 150 us  [per_device(): pl.pallas_call(kernel, out_shape=jax.ShapeDtypeStruct((NC, bs, bs), F32),...]
where the time goes in v2:
time: 154 us; the launch traced here: 153 us
  Pallas kernels  150 us (97%)
  local copies, waits for them, and re-layouts  3.43 us (2%)
    pallas_call x1, Pallas kernels, per_device(): pl.pallas_call(kernel, out_shape=jax.ShapeDtypeStruct((NC, bs, bs), F32),...  150 us
    unnamed x1, local copies, waits for them, and re-layouts  3.43 us

profile of v2, /device:TPU:1, one launch (start us, length us, event | category | flops | bytes accessed | tf_op | source)
XLA Modules:
  0.0 153.4 jit_solution(7221614495680699857)
XLA Ops:
  0.0 150.0 %shard_map.64 = f32[10,256,256]{2,1,0:T(8,128)} custom-call(s32[2,10]{1,0:T(2,128)} %bitcast.15, s32[1,4]{1,0:T(1,128)} %owner_s.1, s32[2,10]{1,0:T(2,128)} %bitcast.16, s32[2,12]{1,0:T(2,128)} %bitcast.17, f32[10,256,256]{2,1,0:T(8,128)} %bitcast.14, f32[12,256,256]{2,1,0:T(8,128)} %bitcast.13), custom_call_target="tpu_custom_call" | custom-call | flops 20000000000 | bytes 10000000 | tf_op jit(solution)/shard_map/pallas_call | solution.py:374
  150.0 3.4 %copy.8 = f32[1,1,10,256,256]{4,3,2,1,0:T(8,128)} copy(f32[1,1,10,256,256]{4,3,2,1,0:T(8,128)} %bitcast.12) | data formatting | bytes 5242880

commit v3 on v2

--- a/solution.py
+++ b/solution.py
@@ -12,7 +12,9 @@
 NS = 10
 NX = 12
 NC = 10
-NT = 4
+ROWS = (64, 80, 64, 48)
+NT = len(ROWS)
+STARTS = tuple(sum(ROWS[:t]) for t in range(NT))
 ND = 6
 NR = 3
 HALF = NS // 2
@@ -22,11 +24,10 @@
 
 
 def kernel(c_s, owner_s, s_places, x_places, s_hbm, x_hbm, o_hbm, *rest):
-    lbufs = rest[:NT]
-    (recv1, r_own, r_a, r_two, r_b, rd_hi, rd_lo, l_dense, acc, out_v, meta_v, group_v, density_v,
-     group_s, density_s, ss, rs, rss, rrs, dss, drs, pss, prs, ms, mr, own_sem, local_sem, out_sem) = rest[NT:]
+    lbufs, accs = rest[:NT], rest[NT : 2 * NT]
+    (recv1, r_own, r_a, r_two, r_b, rd_hi, rd_lo, l_dense, out_v, meta_v, group_v, density_v,
+     group_s, density_s, ss, rs, rss, rrs, dss, drs, pss, prs, ms, mr, own_sem, local_sem, out_sem) = rest[2 * NT :]
     bs = s_hbm.shape[-1]
-    tr = bs // NT
     n_loop, n_bcast = lax.axis_size("loop"), lax.axis_size("bcast")
     l, b = lax.axis_index("loop"), lax.axis_index("bcast")
     core = lax.rem(l, 2)
@@ -73,14 +74,15 @@
         return lbufs[t].at[pl.ds(HALF * slot(dev), HALF)]
 
     def part(t, dev, j):
-        return lbufs[t].at[pl.ds(HALF * slot(dev), HALF), pl.ds(j * (tr // 2), tr // 2)]
+        return lbufs[t].at[pl.ds(HALF * slot(dev), HALF), pl.ds(j * (ROWS[t] // 2), ROWS[t] // 2)]
 
     left, right = down[1], up[1]
 
     def margin(t, kind):
         if kind == 0:
-            src = s_hbm.at[pl.ds(HALF * (1 - half), HALF), pl.ds(t * tr, tr)]
-            return remote(src, recv1.at[t], ss.at[t, 0], rs.at[t, 0], bcast_at(4))
+            rows = pl.ds(STARTS[t], ROWS[t])
+            src = s_hbm.at[pl.ds(HALF * (1 - half), HALF), rows]
+            return remote(src, recv1.at[:, rows], ss.at[t, 0], rs.at[t, 0], bcast_at(4))
         ref, dev = {
             1: (lambda: whole(t, b), across),
             2: (lambda: whole(t, b), up),
@@ -101,9 +103,12 @@
     def density(kind):
         dev, src, dst = {
             1: (lower, x_hbm, r_a),
-            2: (sibling, r_two, r_b),
         }[kind]
         return remote(src, dst, rss.at[kind], rrs.at[kind], dev)
+
+    def shared(j):
+        at = pl.ds(j * xn, xn)
+        return remote(r_two.at[at], r_b.at[at], pss.at[2, j], prs.at[2, j], sibling)
 
     def direct(k):
         at = pl.ds(k * (NX // ND), NX // ND)
@@ -126,7 +131,7 @@
         pl.when(jnp.logical_not(flag))(otherwise)
 
     def own_half(t):
-        src = s_hbm.at[pl.ds(HALF * half, HALF), pl.ds(t * tr, tr)]
+        src = s_hbm.at[pl.ds(HALF * half, HALF), pl.ds(STARTS[t], ROWS[t])]
         return pltpu.make_async_copy(src, whole(t, b), own_sem.at[t])
 
     def begin(t):
@@ -183,7 +188,7 @@
 
         def body(i, carry):
             at = HALF * slot(b) + i
-            lbufs[t][at] = jnp.where(wanted, lbufs[t][at], recv1[t, i])
+            lbufs[t][at] = jnp.where(wanted, lbufs[t][at], recv1[i, STARTS[t] : STARTS[t] + ROWS[t], :])
             return carry
 
         lax.fori_loop(0, HALF, body, 0)
@@ -215,6 +220,16 @@
             direct(k).wait_send()
             direct(k + 2).start()
 
+    def share(j):
+        each = ND // NR
+
+        def direct_in():
+            for k in range(each * j, each * (j + 1)):
+                direct(k).wait_recv()
+
+        either(takes, lambda: relay(j).wait_recv(), direct_in)
+        shared(j).start()
+
     def density_turn(j):
         if j + 1 < NR:
 
@@ -232,7 +247,7 @@
 
     def spread_margin(t):
         for j in range(STEPS):
-            root = owner_s[0, step_of[j]]
+            root, tr = owner_s[0, step_of[j]], ROWS[t]
 
             def body(i, carry):
                 r, k = i // KB, lax.rem(i, KB)
@@ -244,32 +259,34 @@
                 l_dense[t % 2, j, pl.ds(pl.multiple_of((RB + r) * tr, tr), tr), cols] = low
                 return carry
 
-            lax.fori_loop(0, RB * KB, body, 0)
+            lax.fori_loop(0, RB * KB, body, 0, unroll=2)
 
     def multiply(t, terms):
+        tr, acc = ROWS[t], accs[t]
+
         def column(c, carry):
             total = jnp.zeros((RB * tr, bs), F32)
             for j in terms:
-                first = jnp.dot(l_dense[t % 2, j], rd_hi[j, c], preferred_element_type=F32)
+                first = jnp.dot(l_dense[t % 2, j, : 2 * RB * tr, :], rd_hi[j, c], preferred_element_type=F32)
                 second = jnp.dot(l_dense[t % 2, j, : RB * tr, :], rd_lo[j, c], preferred_element_type=F32)
                 total = total + (first[: RB * tr] + (first[RB * tr :] + second))
             for r in range(RB):
                 piece = total[r * tr : (r + 1) * tr]
-                acc[t, r * CB + c] = piece if terms[0] == 0 else acc[t, r * CB + c] + piece
+                acc[r * CB + c] = piece if terms[0] == 0 else acc[r * CB + c] + piece
             return carry
 
         lax.fori_loop(0, CB, column, 0)
 
     def keep(t):
         def body(m, carry):
-            out_v[m, t * tr : (t + 1) * tr, :] = acc[t, c_s[0, m] * CB + c_s[1, m]]
+            out_v[m, STARTS[t] : STARTS[t] + ROWS[t], :] = accs[t][c_s[0, m] * CB + c_s[1, m]]
             return carry
 
         lax.fori_loop(0, NC, body, 0)
         out(t).start()
 
     def out(t):
-        at = pl.ds(t * tr, tr)
+        at = pl.ds(STARTS[t], ROWS[t])
         return pltpu.make_async_copy(out_v.at[:, at], o_hbm.at[:, at], out_sem.at[t])
 
     for i in range(10):
@@ -306,35 +323,29 @@
     advance(3)
     forward_crossed(1)
     density_turn(2)
+    share(0)
     forward_own(2)
+    cross(3)
     finish(0)
-    cross(3)
     pl.when(jnp.logical_not(relays))(lambda: density(1).wait_recv())
     spread_density(r_a, 1, step_of[1])
+    spread_margin(0)
+    multiply(0, (0, 1))
+    share(1)
     forward_crossed(2)
     forward_own(3)
-    spread_margin(0)
-    multiply(0, (0, 1))
+
+    share(2)
+    spread_density(r_two, 2, 2)
     finish(1)
-    forward_crossed(3)
     spread_margin(1)
     multiply(1, (0, 1))
-
-    def parts_in():
-        for j in range(NR):
-            relay(j).wait_recv()
-
-    def direct_in():
-        for k in range(ND):
-            direct(k).wait_recv()
-
-    either(takes, parts_in, direct_in)
-    density(2).start()
-    spread_density(r_two, 2, 2)
-    density(2).wait_recv()
+    for j in range(NR):
+        shared(j).wait_recv()
     spread_density(r_b, 3, step_of[3])
     multiply(0, (2, 3))
     keep(0)
+    forward_crossed(3)
     multiply(1, (2, 3))
     keep(1)
     for t in range(2, NT):
@@ -347,7 +358,8 @@
         out(t).wait()
         for kind in range(10):
             margin(t, kind).wait_send()
-    density(2).wait_send()
+    for j in range(NR):
+        shared(j).wait_send()
 
     def sent():
         density(1).wait_send()
@@ -367,7 +379,6 @@
 
 def per_device(s_blocks, s_list, x_blocks, x_list, c_list, owner):
     bs = s_blocks.shape[-1]
-    tr = bs // NT
     smem = pl.BlockSpec(memory_space=pltpu.SMEM)
     vmem = pl.BlockSpec(memory_space=pltpu.VMEM)
     hbm = pl.BlockSpec(memory_space=pltpu.HBM)
@@ -376,16 +387,17 @@
         out_shape=jax.ShapeDtypeStruct((NC, bs, bs), F32),
         in_specs=[smem, smem, vmem, vmem, hbm, hbm],
         out_specs=hbm,
-        scratch_shapes=[pltpu.VMEM((4 * NS, tr, bs), F32)] * NT + [
-            pltpu.VMEM((NT, HALF, tr, bs), F32),
+        scratch_shapes=[
+            *(pltpu.VMEM((4 * NS, tr, bs), F32) for tr in ROWS),
+            *(pltpu.VMEM((RB * CB, tr, bs), F32) for tr in ROWS),
+            pltpu.VMEM((HALF, bs, bs), F32),
             pltpu.VMEM((NX, bs, bs), F32),
             pltpu.VMEM((NX, bs, bs), F32),
             pltpu.VMEM((NX, bs, bs), F32),
             pltpu.VMEM((NX, bs, bs), F32),
             pltpu.VMEM((STEPS, CB, KB * bs, bs), BF16),
             pltpu.VMEM((STEPS, CB, KB * bs, bs), BF16),
-            pltpu.VMEM((2, STEPS, 2 * RB * tr, KB * bs), BF16),
-            pltpu.VMEM((NT, RB * CB, tr, bs), F32),
+            pltpu.VMEM((2, STEPS, 2 * RB * max(ROWS), KB * bs), BF16),
             pltpu.VMEM((NC, bs, bs), F32),
             pltpu.VMEM((KB * CB, 128), jnp.int32),
             pltpu.VMEM((8, KB * CB, 128), jnp.int32),
@@ -394,12 +406,12 @@
             pltpu.SMEM((4, KB * CB, 128), jnp.int32),
             pltpu.SemaphoreType.DMA((NT, 10)),
             pltpu.SemaphoreType.DMA((NT, 10)),
-            pltpu.SemaphoreType.DMA((3,)),
-            pltpu.SemaphoreType.DMA((3,)),
+            pltpu.SemaphoreType.DMA((2,)),
+            pltpu.SemaphoreType.DMA((2,)),
             pltpu.SemaphoreType.DMA((ND,)),
             pltpu.SemaphoreType.DMA((ND,)),
-            pltpu.SemaphoreType.DMA((2, NR)),
-            pltpu.SemaphoreType.DMA((2, NR)),
+            pltpu.SemaphoreType.DMA((3, NR)),
+            pltpu.SemaphoreType.DMA((3, NR)),
             pltpu.SemaphoreType.DMA((10,)),
             pltpu.SemaphoreType.DMA((10,)),
             pltpu.SemaphoreType.DMA((NT,)),

time: 154 us -> 141 us (0.916)
  Pallas kernels: 150 us -> 137 us
    pallas_call x1, Pallas kernels: 150 us -> 137 us  [per_device(): pl.pallas_call(kernel, out_shape=jax.ShapeDtypeStruct((NC, bs, bs), F32),...]
where the time goes in v3:
time: 141 us; the launch traced here: 140 us
  Pallas kernels  137 us (97%)
  local copies, waits for them, and re-layouts  3.43 us (2%)
    pallas_call x1, Pallas kernels, per_device(): pl.pallas_call(kernel, out_shape=jax.ShapeDtypeStruct((NC, bs, bs), F32),...  137 us
    unnamed x1, local copies, waits for them, and re-layouts  3.43 us

profile of v3, /device:TPU:1, one launch (start us, length us, event | category | flops | bytes accessed | tf_op | source)
XLA Modules:
  0.0 140.3 jit_solution(2547564860609760341)
XLA Ops:
  0.0 136.9 %shard_map.64 = f32[10,256,256]{2,1,0:T(8,128)} custom-call(s32[2,10]{1,0:T(2,128)} %bitcast.15, s32[1,4]{1,0:T(1,128)} %owner_s.1, s32[2,10]{1,0:T(2,128)} %bitcast.16, s32[2,12]{1,0:T(2,128)} %bitcast.17, f32[10,256,256]{2,1,0:T(8,128)} %bitcast.14, f32[12,256,256]{2,1,0:T(8,128)} %bitcast.13), custom_call_target="tpu_custom_call" | custom-call | flops 20000000000 | bytes 10000000 | tf_op jit(solution)/shard_map/pallas_call | solution.py:385
  136.9 3.4 %copy.8 = f32[1,1,10,256,256]{4,3,2,1,0:T(8,128)} copy(f32[1,1,10,256,256]{4,3,2,1,0:T(8,128)} %bitcast.12) | data formatting | bytes 5242880

commit v4 on v3

--- a/solution.py
+++ b/solution.py
@@ -144,6 +144,8 @@
         by = i - 6
         return remote(meta_v, density_v.at[by], ms.at[i], mr.at[i], loop_at(-by))
 
+    begin(0)
+    begin(1)
     for i in range(10):
         table(i).start()
     mine_g = pltpu.make_async_copy(meta_v, group_v.at[b], local_sem.at[1])
@@ -151,7 +153,6 @@
     mine_g.start()
     mine_d.start()
 
-    begin(0)
     either(gives, lambda: relayed(0).start(), lambda: density(1).start())
 
     @pl.when(jnp.logical_not(gives))
@@ -159,7 +160,6 @@
         direct(0).start()
         direct(1).start()
 
-    begin(1)
     own_density = pltpu.make_async_copy(x_hbm, r_own, local_sem.at[0])
     own_density.start()
 
@@ -259,7 +259,7 @@
                 l_dense[t % 2, j, pl.ds(pl.multiple_of((RB + r) * tr, tr), tr), cols] = low
                 return carry
 
-            lax.fori_loop(0, RB * KB, body, 0, unroll=2)
+            lax.fori_loop(0, RB * KB, body, 0, unroll=4)
 
     def multiply(t, terms):
         tr, acc = ROWS[t], accs[t]
@@ -289,6 +289,12 @@
         at = pl.ds(STARTS[t], ROWS[t])
         return pltpu.make_async_copy(out_v.at[:, at], o_hbm.at[:, at], out_sem.at[t])
 
+    choose(0)
+    begin(2)
+    advance(0)
+    choose(1)
+    begin(3)
+    cross(0)
     for i in range(10):
         table(i).wait_recv()
     mine_g.wait()
@@ -299,19 +305,13 @@
     ]
     for copy in to_s:
         copy.start()
-    choose(0)
-    begin(2)
-    advance(0)
-    choose(1)
-    begin(3)
-    for copy in to_s:
-        copy.wait()
-    cross(0)
     density_turn(0)
     advance(1)
     forward_own(0)
     choose(2)
     cross(1)
+    for copy in to_s:
+        copy.wait()
     own_density.wait()
     spread_density(r_own, 0, 0)
     advance(2)

time: 141 us -> 141 us (level)
  no operation moved by 1% of the time
where the time goes in v4:
time: 141 us; the launch traced here: 140 us
  Pallas kernels  137 us (97%)
  local copies, waits for them, and re-layouts  3.43 us (2%)
    pallas_call x1, Pallas kernels, per_device(): pl.pallas_call(kernel, out_shape=jax.ShapeDtypeStruct((NC, bs, bs), F32),...  137 us
    unnamed x1, local copies, waits for them, and re-layouts  3.43 us

profile of v4, /device:TPU:1, one launch (start us, length us, event | category | flops | bytes accessed | tf_op | source)
XLA Modules:
  0.0 140.0 jit_solution(16063247157777954132)
XLA Ops:
  0.0 136.6 %shard_map.64 = f32[10,256,256]{2,1,0:T(8,128)} custom-call(s32[2,10]{1,0:T(2,128)} %bitcast.15, s32[1,4]{1,0:T(1,128)} %owner_s.1, s32[2,10]{1,0:T(2,128)} %bitcast.16, s32[2,12]{1,0:T(2,128)} %bitcast.17, f32[10,256,256]{2,1,0:T(8,128)} %bitcast.14, f32[12,256,256]{2,1,0:T(8,128)} %bitcast.13), custom_call_target="tpu_custom_call" | custom-call | flops 20000000000 | bytes 10000000 | tf_op jit(solution)/shard_map/pallas_call | solution.py:385
  136.6 3.4 %copy.8 = f32[1,1,10,256,256]{4,3,2,1,0:T(8,128)} copy(f32[1,1,10,256,256]{4,3,2,1,0:T(8,128)} %bitcast.12) | data formatting | bytes 5242880

commit v5 on v4

--- a/solution.py
+++ b/solution.py
@@ -178,7 +178,7 @@
             rd_lo[j, c, rows, :] = low
             return carry
 
-        lax.fori_loop(0, KB * CB, body, 0)
+        lax.fori_loop(0, KB * CB, body, 0, unroll=2)
 
     wanted = (owner_s[0, 0] == b) | (owner_s[0, 1] == b) | (owner_s[0, 2] == b) | (owner_s[0, 3] == b)
 
@@ -282,7 +282,7 @@
             out_v[m, STARTS[t] : STARTS[t] + ROWS[t], :] = accs[t][c_s[0, m] * CB + c_s[1, m]]
             return carry
 
-        lax.fori_loop(0, NC, body, 0)
+        lax.fori_loop(0, NC, body, 0, unroll=5)
         out(t).start()
 
     def out(t):

time: 141 us -> 140 us (level)
  no operation moved by 1% of the time
where the time goes in v5:
time: 140 us
  Pallas kernels  136 us (97%)
  local copies, waits for them, and re-layouts  3.43 us (2%)
    pallas_call x1, Pallas kernels, per_device(): pl.pallas_call(kernel, out_shape=jax.ShapeDtypeStruct((NC, bs, bs), F32),...  136 us
    unnamed x1, local copies, waits for them, and re-layouts  3.43 us

profile of v5, /device:TPU:1, one launch (start us, length us, event | category | flops | bytes accessed | tf_op | source)
XLA Modules:
  0.0 139.8 jit_solution(5179971959027366863)
XLA Ops:
  0.0 136.3 %shard_map.64 = f32[10,256,256]{2,1,0:T(8,128)} custom-call(s32[2,10]{1,0:T(2,128)} %bitcast.15, s32[1,4]{1,0:T(1,128)} %owner_s.1, s32[2,10]{1,0:T(2,128)} %bitcast.16, s32[2,12]{1,0:T(2,128)} %bitcast.17, f32[10,256,256]{2,1,0:T(8,128)} %bitcast.14, f32[12,256,256]{2,1,0:T(8,128)} %bitcast.13), custom_call_target="tpu_custom_call" | custom-call | flops 20000000000 | bytes 10000000 | tf_op jit(solution)/shard_map/pallas_call | solution.py:385
  136.3 3.4 %copy.8 = f32[1,1,10,256,256]{4,3,2,1,0:T(8,128)} copy(f32[1,1,10,256,256]{4,3,2,1,0:T(8,128)} %bitcast.12) | data formatting | bytes 5242880
